TPU v7x, 32 devices: a whole 2x2x4 slice. The times are simulated.
32 devices in a mesh: pool: 2 (over x), hold: 8 (over z, y), head: 2 (over core).
Axes of the slice: x: 2, y: 2, z: 4, core: 2. Of those that a mesh axis runs over, the one named last changes fastest.
Arguments:
- query_nope: bfloat16 [2048, 32, 128], P(('pool', 'hold'), 'head'), parts along dimension 0, may hold values from -6 to 6
- query_rope: bfloat16 [2048, 2048], P(('pool', 'hold'), 'head'), parts along dimension 0, may hold values from -8 to 8
- key_up: bfloat16 [32, 128, 512], P('head'), may hold values from -0.5 to 0.5
- value_up: bfloat16 [32, 512, 128], P('head'), may hold values from -3 to 3
- span_latent: bfloat16 [2048, 512], P(('pool', 'hold')), parts along dimension 0, may hold values from -6 to 6
- span_rope: bfloat16 [64, 2048], P(None, ('pool', 'hold')), parts along dimension 1, may hold values from -8 to 8
- pool_latent: bfloat16 [96, 128, 512], P(('pool', 'hold')), parts along dimension 0, may hold values from -6 to 6
- pool_rope: bfloat16 [96, 64, 128], P(('pool', 'hold')), parts along dimension 0, may hold values from -6 to 6
- hit_holders: int32 [16, 24], P(('pool', 'hold')), parts along dimension 0, may hold values from 0 to 7, as said below
- hit_blocks: int32 [16, 24], P(('pool', 'hold')), parts along dimension 0, may hold values from 0 to 5, as said below
- prefix_len: int32 [16], P(('pool', 'hold')), parts along dimension 0, may hold values from 2305 to 3072, as said below
- span_len: int32 [16], P(('pool', 'hold')), parts along dimension 0, may hold values from 64 to 128, as said below
Outputs:
- attended: bfloat16 [2048, 4096], P(('pool', 'hold'), 'head'), parts along dimension 0
There are 2 independent parts, one for each index of `pool`. A program takes and returns all parts, laid end to end along the dimension named above; an argument that names none is the same for every part. Nothing has to cross between parts.
Inputs may be any that keep to these rules, and one draw needn't show every extreme that they name: `hit_holders`: among one request's 24 entries at most 3 name the same device; in every draw some request takes exactly 3 blocks from one device. `hit_blocks`: entries of one request on one device name distinct slots; different requests may share blocks. `prefix_len`: some request has the full 24 * 128 tokens in every draw. `span_len`: some request has all 128 tokens in every draw.
All inputs are finite; a program needn't handle non-finite values.
Results may differ from a plain program's by a relative error of at most 0.0095.
Values may be sent and summed in bfloat16 or wider, within the bound.
A program may use at most 64 MiB of HBM per device.

v0:
```python
import functools
import math

import jax
import jax.numpy as jnp
from jax import lax
from jax.experimental import pallas as pl
from jax.experimental.pallas import tpu as pltpu
from jax.sharding import PartitionSpec as P

MESH = pl.DeviceIdType.MESH
MASKED = -1e30


def send_order(holders):
    near = list(range(1, holders // 2))
    far = list(range(holders // 2, holders))
    order = []
    while near or far:
        if near:
            order.append(near.pop(0))
        if far:
            order.append(far.pop(0))
    return order


def kernel(
    sizes,
    table_ref,
    bias_ref,
    count_ref,
    pool_lat,
    pool_rope,
    span_lat,
    span_rope,
    nope_hbm,
    rope_q,
    key_up_hbm,
    value_up_hbm,
    out_ref,
    table_in,
    table_smem,
    send_lat,
    send_rope,
    kv,
    kr,
    nope,
    nope32,
    key_up,
    value_up,
    q_lat,
    q_aug,
    acc,
    peak,
    total,
    local_sem,
    table_send,
    table_recv,
    lat_send,
    lat_recv,
    rope_send,
    rope_recv,
    fwd_lat_send,
    fwd_lat_recv,
    fwd_rope_send,
    fwd_rope_recv,
):
    holders, slots, heads, toks, block, lat, rope, scale = sizes
    width = slots * block
    half = lat // 2
    rope_half = rope // 2
    pool, me, core = lax.axis_index("pool"), lax.axis_index("hold"), lax.axis_index("head")
    other = 1 - core
    sibling = (pool, me, other)
    order = send_order(holders)
    base = {0: toks}
    for at, k in enumerate(order):
        base[k] = toks + (at + 1) * width

    def peer(k):
        return (pool, me ^ k, core)

    loads = [
        pltpu.make_async_copy(nope_hbm, nope, local_sem.at[0]),
        pltpu.make_async_copy(key_up_hbm, key_up, local_sem.at[1]),
        pltpu.make_async_copy(value_up_hbm, value_up, local_sem.at[2]),
    ]
    for load in loads:
        load.start()

    barrier = pltpu.get_barrier_semaphore()
    for k in order:
        pl.semaphore_signal(barrier, inc=1, device_id=peer(k), device_id_type=MESH)
    pl.semaphore_signal(barrier, inc=1, device_id=sibling, device_id_type=MESH)
    pl.semaphore_wait(barrier, holders)

    tables = []
    for k in order:
        copy = pltpu.make_async_remote_copy(
            src_ref=table_ref.at[me ^ k],
            dst_ref=table_in.at[k],
            send_sem=table_send.at[k],
            recv_sem=table_recv.at[k],
            device_id=peer(k),
            device_id_type=MESH,
        )
        copy.start()
        tables.append(copy)
    table_in[0] = table_ref[me]
    for copy in tables:
        copy.wait_recv()
    to_smem = pltpu.make_async_copy(table_in, table_smem, local_sem.at[3])
    to_smem.start()
    to_smem.wait()

    copies = {}
    for k in order:
        for s in range(slots):
            b = table_smem[k, 0, s]
            rows = pl.ds(s * block, block)
            send_lat[k, rows, :] = pool_lat[b, :, pl.ds(pl.multiple_of(core * half, half), half)]
            send_rope[k, :, rows] = pool_rope[
                b, pl.ds(pl.multiple_of(core * rope_half, rope_half), rope_half), :
            ]
        lat_copy = pltpu.make_async_remote_copy(
            src_ref=send_lat.at[k],
            dst_ref=kv.at[core, pl.ds(base[k], width), :],
            send_sem=lat_send.at[k],
            recv_sem=lat_recv.at[k],
            device_id=peer(k),
            device_id_type=MESH,
        )
        rope_copy = pltpu.make_async_remote_copy(
            src_ref=send_rope.at[k],
            dst_ref=kr.at[
                pl.ds(pl.multiple_of(core * rope_half, rope_half), rope_half), pl.ds(base[k], width)
            ],
            send_sem=rope_send.at[k],
            recv_sem=rope_recv.at[k],
            device_id=peer(k),
            device_id_type=MESH,
        )
        lat_copy.start()
        rope_copy.start()
        copies[k] = (lat_copy, rope_copy)

    for c in range(2):
        kv[c, pl.ds(0, toks), :] = span_lat[:, c * half : (c + 1) * half]
    kr[pl.ds(0, rope), pl.ds(0, toks)] = span_rope[...]
    kr[pl.ds(rope, 128 - rope), :] = jnp.zeros((128 - rope, kr.shape[1]), jnp.bfloat16)
    for s in range(slots):
        b = table_smem[0, 0, s]
        for c in range(2):
            kv[c, pl.ds(toks + s * block, block), :] = pool_lat[b, :, c * half : (c + 1) * half]
        kr[pl.ds(0, rope), pl.ds(toks + s * block, block)] = pool_rope[b]
    for k in [0] + order:
        kr[pl.ds(rope, 16), pl.ds(base[k], width)] = bias_ref[me ^ k]

    loads[0].wait()
    loads[1].wait()
    nope32[...] = nope[...].astype(jnp.float32)
    one_col = (lax.broadcasted_iota(jnp.int32, (toks, 128 - rope), 1) == 0).astype(jnp.bfloat16)
    for h in range(heads):
        q_h = nope32[pl.ds(h, toks, stride=heads), :].astype(jnp.bfloat16)
        up = jnp.dot(q_h, key_up[h], preferred_element_type=jnp.float32)
        q_lat[pl.ds(h * toks, toks), :] = (up * scale).astype(jnp.bfloat16)
        rot = rope_q[:, h * rope : (h + 1) * rope].astype(jnp.float32) * scale
        q_aug[pl.ds(h * toks, toks), :] = jnp.concatenate([rot.astype(jnp.bfloat16), one_col], axis=1)

    tile = 2 * toks
    tiles = heads // 2
    nt = (((1,), (1,)), ((), ()))

    def attend(start, size, first):
        keys = pl.ds(start, size)

        def one(t, carry):
            rows = pl.ds(pl.multiple_of(t * tile, tile), tile)
            s = lax.dot_general(
                q_lat[rows, 0:half], kv[0, keys, :], nt, preferred_element_type=jnp.float32
            )
            s += lax.dot_general(
                q_lat[rows, half:lat], kv[1, keys, :], nt, preferred_element_type=jnp.float32
            )
            s += jnp.dot(q_aug[rows, :], kr[:, keys], preferred_element_type=jnp.float32)
            if first:
                row = lax.broadcasted_iota(jnp.int32, (tile, size), 0) % toks
                col = lax.broadcasted_iota(jnp.int32, (tile, size), 1)
                s = jnp.where((col <= row) | (col >= toks), s, MASKED)
            top = jnp.max(s, axis=1, keepdims=True)
            if not first:
                old = peak[rows, :]
                top = jnp.maximum(top, old)
                alpha = jnp.exp2(old - top)
            p = jnp.exp2(s - top)
            summed = jnp.sum(p, axis=1, keepdims=True)
            p = p.astype(jnp.bfloat16)
            peak[rows, :] = top
            total[rows, :] = summed if first else total[rows, :] * alpha + summed
            for c in range(2):
                cols = pl.ds(c * half, half)
                mixed = jnp.dot(p, kv[c, keys, :], preferred_element_type=jnp.float32)
                acc[rows, cols] = mixed if first else acc[rows, cols] * alpha + mixed
            return carry

        lax.fori_loop(0, tiles, one, 0, unroll=2)

    attend(0, toks + width, True)

    forwards = []
    group = max(1, 768 // width)
    for at in range(0, len(order), group):
        members = order[at : at + group]
        current = []
        for k in members:
            copies[k][0].wait_recv()
            copies[k][1].wait_recv()
            lat_rows = kv.at[core, pl.ds(base[k], width), :]
            rope_rows = kr.at[
                pl.ds(pl.multiple_of(core * rope_half, rope_half), rope_half), pl.ds(base[k], width)
            ]
            lat_fwd = pltpu.make_async_remote_copy(
                src_ref=lat_rows,
                dst_ref=lat_rows,
                send_sem=fwd_lat_send.at[k],
                recv_sem=fwd_lat_recv.at[k],
                device_id=sibling,
                device_id_type=MESH,
            )
            rope_fwd = pltpu.make_async_remote_copy(
                src_ref=rope_rows,
                dst_ref=rope_rows,
                send_sem=fwd_rope_send.at[k],
                recv_sem=fwd_rope_recv.at[k],
                device_id=sibling,
                device_id_type=MESH,
            )
            lat_fwd.start()
            rope_fwd.start()
            current += [lat_fwd, rope_fwd]
        for copy in current:
            copy.wait_recv()
        forwards += current
        attend(base[members[0]], len(members) * width, False)

    loads[2].wait()
    live = lax.broadcasted_iota(jnp.int32, (toks, value_up.shape[2]), 0) < count_ref[0]
    for h in range(heads):
        rows = pl.ds(h * toks, toks)
        mixed = (acc[rows, :] / total[rows, :]).astype(jnp.bfloat16)
        up = jnp.dot(mixed, value_up[h], preferred_element_type=jnp.float32)
        vdim = value_up.shape[2]
        out_ref[:, h * vdim : (h + 1) * vdim] = jnp.where(live, up, 0.0).astype(out_ref.dtype)

    for copy in tables + forwards:
        copy.wait_send()
    for k in order:
        copies[k][0].wait_send()
        copies[k][1].wait_send()


def on_device(
    query_nope,
    query_rope,
    key_up,
    value_up,
    span_latent,
    span_rope,
    pool_latent,
    pool_rope,
    hit_holders,
    hit_blocks,
    prefix_len,
    span_len,
):
    holders = lax.axis_size("hold")
    toks, heads, nope_width = query_nope.shape
    lat = key_up.shape[2]
    rope = span_rope.shape[0]
    block = pool_latent.shape[1]
    list_len = hit_holders.shape[1]
    vdim = value_up.shape[2]
    slots = (list_len + holders - 1) // holders
    width = slots * block
    scale = float(nope_width + rope) ** (-0.5) * math.log2(math.e)

    row = hit_holders[0]
    entry = jnp.arange(list_len)
    rank = jnp.sum((row[:, None] == row[None, :]) & (entry[None, :] < entry[:, None]), axis=1)
    match = (row[None, None, :] == jnp.arange(holders)[:, None, None]) & (
        rank[None, None, :] == jnp.arange(slots)[None, :, None]
    )
    ids = jnp.sum(jnp.where(match, hit_blocks[0][None, None, :], 0), axis=2)
    table = jnp.broadcast_to(
        jnp.pad(ids, ((0, 0), (0, 128 - slots)))[:, None, :], (holders, 8, 128)
    ).astype(jnp.int32)
    seen = jnp.sum(jnp.where(match, jnp.maximum(prefix_len[0] - entry * block, 0), 0), axis=2)
    hidden = jnp.arange(block)[None, None, :] >= seen[:, :, None]
    bias = jnp.where(hidden, MASKED, 0.0).reshape(holders, 1, width)
    first_row = jnp.arange(16)[None, :, None] == 0
    bias = jnp.where(first_row, bias, 0.0).astype(jnp.bfloat16)

    keys = toks + holders * width
    rows = heads * toks
    vmem = pl.BlockSpec(memory_space=pltpu.VMEM)
    any_space = pl.BlockSpec(memory_space=pl.ANY)
    sems = pltpu.SemaphoreType.DMA((holders,))
    sizes = (holders, slots, heads, toks, block, lat, rope, scale)
    return pl.pallas_call(
        functools.partial(kernel, sizes),
        out_shape=jax.ShapeDtypeStruct((toks, heads * vdim), jnp.bfloat16),
        in_specs=[
            vmem,
            vmem,
            pl.BlockSpec(memory_space=pltpu.SMEM),
            vmem,
            vmem,
            vmem,
            vmem,
            any_space,
            vmem,
            any_space,
            any_space,
        ],
        out_specs=vmem,
        scratch_shapes=[
            pltpu.VMEM((holders, 8, 128), jnp.int32),
            pltpu.SMEM((holders, 8, 128), jnp.int32),
            pltpu.VMEM((holders, width, lat // 2), jnp.bfloat16),
            pltpu.VMEM((holders, rope // 2, width), jnp.bfloat16),
            pltpu.VMEM((2, keys, lat // 2), jnp.bfloat16),
            pltpu.VMEM((128, keys), jnp.bfloat16),
            pltpu.VMEM((rows, nope_width), jnp.bfloat16),
            pltpu.VMEM((rows, nope_width), jnp.float32),
            pltpu.VMEM(key_up.shape, jnp.bfloat16),
            pltpu.VMEM(value_up.shape, jnp.bfloat16),
            pltpu.VMEM((rows, lat), jnp.bfloat16),
            pltpu.VMEM((rows, 128), jnp.bfloat16),
            pltpu.VMEM((rows, lat), jnp.float32),
            pltpu.VMEM((rows, 1), jnp.float32),
            pltpu.VMEM((rows, 1), jnp.float32),
            pltpu.SemaphoreType.DMA((4,)),
        ]
        + [sems] * 10,
        compiler_params=pltpu.CompilerParams(
            collective_id=0, has_side_effects=True, vmem_limit_bytes=48 * 1024 * 1024
        ),
    )(
        table,
        bias,
        span_len,
        pool_latent,
        pool_rope,
        span_latent,
        span_rope,
        query_nope.reshape(rows, nope_width),
        query_rope,
        key_up,
        value_up,
    )


def solution(mesh):
    return jax.shard_map(
        on_device,
        mesh=mesh,
        in_specs=(
            P(("pool", "hold"), "head", None),
            P(("pool", "hold"), "head"),
            P("head", None, None),
            P("head", None, None),
            P(("pool", "hold"), None),
            P(None, ("pool", "hold")),
            P(("pool", "hold"), None, None),
            P(("pool", "hold"), None, None),
            P(("pool", "hold"), None),
            P(("pool", "hold"), None),
            P(("pool", "hold")),
            P(("pool", "hold")),
        ),
        out_specs=P(("pool", "hold"), "head"),
        check_vma=False,
    )
```

profile of v0, /device:TPU:0, one launch (start us, length us, event | category | flops | bytes accessed | tf_op | source)
XLA Modules:
  0.0 83.7 jit_solution(12110162402074547134)
XLA Ops:
  1.3 0.9 %convert_reduce_fusion = s32[24]{0:T(128)S(1)} fusion(s32[24]{0:T(128)} %bitcast.13), kind=kLoop, calls=%fused_computation.6 | loop fusion | flops 2856 | bytes 192 | tf_op jit(solution)/shard_map/reduce_sum | solution.py:289
  2.2 0.7 iota_compare_fusion.1
  2.9 0.8 %fusion.1 = (s32[8,3]{0,1:T(4,128)S(1)}, s32[8,3]{0,1:T(4,128)S(1)}) fusion(s32[24]{0:T(128)S(1)} %subtract_maximum_fusion, pred[3,24]{1,0:T(4,128)(4,1)S(1)} %iota_compare_fusion.2, pred[8,24]{1,0:T(8,128)(4,1)S(1)} %iota_compare_fusion.1, s32[24]{0:T(128)} %bitcast.12), kind=kLoop, calls=%fused_computation.4 | loop fusion | flops 2832 | bytes 648 | tf_op jit(solution)/shard_map/reduce_sum | solution.py:297
  3.7 0.1 fusion.3
  3.8 0.1 copy.14
  3.9 0.1 select_convert_fusion.bias_ref
  4.0 0.0 copy-start
  4.0 1.6 %copy-done = bf16[16,128,512]{2,1,0:T(8,128)(2,1)S(1)} copy-done((bf16[16,128,512]{2,1,0:T(8,128)(2,1)S(1)}, bf16[16,128,512]{2,1,0:T(8,128)(2,1)}, u32[]{:S(2)}) %copy-start) | copy-done | bytes 2097176
  5.6 0.0 copy-start.1
  5.6 1.1 %copy-done.1 = bf16[6,128,512]{2,1,0:T(8,128)(2,1)S(1)} copy-done((bf16[6,128,512]{2,1,0:T(8,128)(2,1)S(1)}, bf16[6,128,512]{2,1,0:T(8,128)(2,1)}, u32[]{:S(2)}) %copy-start.1) | copy-done | bytes 786456
  6.7 0.0 copy-start.2
  6.7 1.0 %copy-done.2 = bf16[128,16,128]{2,1,0:T(8,128)(2,1)S(1)} copy-done((bf16[128,16,128]{2,1,0:T(8,128)(2,1)S(1)}, bf16[128,16,128]{2,1,0:T(8,128)(2,1)}, u32[]{:S(2)}) %copy-start.2) | copy-done | bytes 524312
  7.8 0.0 copy-start.3
  7.8 0.9 %copy-done.3 = bf16[128,1024]{1,0:T(8,128)(2,1)S(1)} copy-done((bf16[128,1024]{1,0:T(8,128)(2,1)S(1)}, bf16[128,1024]{1,0:T(8,128)(2,1)}, u32[]{:S(2)}) %copy-start.3) | copy-done | bytes 262168
  8.7 0.0 copy-start.4
  8.7 0.9 %copy-done.4 = bf16[128,512]{1,0:T(8,128)(2,1)S(1)} copy-done((bf16[128,512]{1,0:T(8,128)(2,1)S(1)}, bf16[128,512]{1,0:T(8,128)(2,1)}, u32[]{:S(2)}) %copy-start.4) | copy-done | bytes 131096
  9.6 0.0 copy-start.5
  9.6 0.9 %copy-done.5 = bf16[6,64,128]{2,1,0:T(8,128)(2,1)S(1)} copy-done((bf16[6,64,128]{2,1,0:T(8,128)(2,1)S(1)}, bf16[6,64,128]{2,1,0:T(8,128)(2,1)}, u32[]{:S(2)}) %copy-start.5) | copy-done | bytes 98328
  10.5 0.0 copy-start.6
  10.5 0.7 copy-done.6
  11.2 71.6 %shard_map.118 = bf16[128,2048]{1,0:T(8,128)(2,1)S(1)} custom-call(s32[8,8,128]{2,1,0:T(8,128)S(1)} %broadcast_in_dim.65.table_ref, bf16[8,16,384]{2,1,0:T(8,128)(2,1)S(1)} %select_convert_fusion.bias_ref, s32[1]{0:T(128)S(6)} %copy.17.count_ref, bf16[6,128,512]{2,1,0:T(8,128)(2,1)S(1)} %copy-done.1, bf16[6,64,128]{2,1,0:T(8,128)(2,1)S(1)} %copy-done.5, ...), custom_call_target="tpu_custom_call" | custom-call | tf_op jit(solution)/shard_map/pallas_call | solution.py:309
  82.9 0.8 copy.18
  (6 shorter events, 0.0 us)
Async XLA Ops:
  4.0 1.6 %copy-start = (bf16[16,128,512]{2,1,0:T(8,128)(2,1)S(1)}, bf16[16,128,512]{2,1,0:T(8,128)(2,1)}, u32[]{:S(2)}) copy-start(bf16[16,128,512]{2,1,0:T(8,128)(2,1)} %key_up_hbm.1) | copy-start | bytes 6291460
  5.6 1.1 %copy-start.1 = (bf16[6,128,512]{2,1,0:T(8,128)(2,1)S(1)}, bf16[6,128,512]{2,1,0:T(8,128)(2,1)}, u32[]{:S(2)}) copy-start(bf16[6,128,512]{2,1,0:T(8,128)(2,1)} %pool_lat.1) | copy-start | bytes 2359300
  6.7 1.0 %copy-start.2 = (bf16[128,16,128]{2,1,0:T(8,128)(2,1)S(1)}, bf16[128,16,128]{2,1,0:T(8,128)(2,1)}, u32[]{:S(2)}) copy-start(bf16[128,16,128]{2,1,0:T(8,128)(2,1)} %param.12) | copy-start | bytes 1572868
  7.8 0.9 %copy-start.3 = (bf16[128,1024]{1,0:T(8,128)(2,1)S(1)}, bf16[128,1024]{1,0:T(8,128)(2,1)}, u32[]{:S(2)}) copy-start(bf16[128,1024]{1,0:T(8,128)(2,1)} %rope_q.1) | copy-start | bytes 786436
  8.7 0.9 %copy-start.4 = (bf16[128,512]{1,0:T(8,128)(2,1)S(1)}, bf16[128,512]{1,0:T(8,128)(2,1)}, u32[]{:S(2)}) copy-start(bf16[128,512]{1,0:T(8,128)(2,1)} %span_lat.1) | copy-start | bytes 393220
  9.6 0.9 %copy-start.5 = (bf16[6,64,128]{2,1,0:T(8,128)(2,1)S(1)}, bf16[6,64,128]{2,1,0:T(8,128)(2,1)}, u32[]{:S(2)}) copy-start(bf16[6,64,128]{2,1,0:T(8,128)(2,1)} %pool_rope.1) | copy-start | bytes 294916
  10.5 0.7 copy-start.6
where the time goes:
time: 85.1 us; the launch traced here: 83.7 us
  Pallas kernels  71.6 us (84%)
  local copies, waits for them, and re-layouts  8.12 us (10%)
  other arithmetic  2.59 us (3%)
  between operations  1.34 us (2%)
    pallas_call x1, Pallas kernels, on_device(): pl.pallas_call(functools.partial(kernel, sizes), out_shape=jax.ShapeDtype...  71.6 us
    unnamed x16, local copies, waits for them, and re-layouts  8.1 us

commit v1 on v0

--- a/solution.py
+++ b/solution.py
@@ -26,30 +26,36 @@
 
 def kernel(
     sizes,
+    table_hbm,
+    bias_hbm,
+    count_ref,
+    pool_lat_hbm,
+    pool_rope_hbm,
+    span_lat_hbm,
+    span_rope_hbm,
+    nope_hbm,
+    rope_q_hbm,
+    key_up_hbm,
+    value_up_hbm,
+    out_ref,
     table_ref,
     bias_ref,
-    count_ref,
     pool_lat,
     pool_rope,
     span_lat,
     span_rope,
-    nope_hbm,
     rope_q,
-    key_up_hbm,
-    value_up_hbm,
-    out_ref,
     table_in,
     table_smem,
     send_lat,
     send_rope,
     kv,
-    kr,
+    kt,
     nope,
     nope32,
     key_up,
     value_up,
-    q_lat,
-    q_aug,
+    q_all,
     acc,
     peak,
     total,
@@ -72,6 +78,7 @@
     pool, me, core = lax.axis_index("pool"), lax.axis_index("hold"), lax.axis_index("head")
     other = 1 - core
     sibling = (pool, me, other)
+    kr = kt.at[pl.ds(lat, 128), :]
     order = send_order(holders)
     base = {0: toks}
     for at, k in enumerate(order):
@@ -80,13 +87,23 @@
     def peer(k):
         return (pool, me ^ k, core)
 
-    loads = [
-        pltpu.make_async_copy(nope_hbm, nope, local_sem.at[0]),
-        pltpu.make_async_copy(key_up_hbm, key_up, local_sem.at[1]),
-        pltpu.make_async_copy(value_up_hbm, value_up, local_sem.at[2]),
+    pairs = [
+        (table_hbm, table_ref),
+        (pool_lat_hbm, pool_lat),
+        (pool_rope_hbm, pool_rope),
+        (span_lat_hbm, span_lat),
+        (span_rope_hbm, span_rope),
+        (bias_hbm, bias_ref),
+        (nope_hbm, nope),
+        (key_up_hbm, key_up),
+        (rope_q_hbm, rope_q),
+        (value_up_hbm, value_up),
     ]
-    for load in loads:
+    loads = []
+    for at, (src, dst) in enumerate(pairs):
+        load = pltpu.make_async_copy(src, dst, local_sem.at[at])
         load.start()
+        loads.append(load)
 
     barrier = pltpu.get_barrier_semaphore()
     for k in order:
@@ -94,6 +111,7 @@
     pl.semaphore_signal(barrier, inc=1, device_id=sibling, device_id_type=MESH)
     pl.semaphore_wait(barrier, holders)
 
+    loads[0].wait()
     tables = []
     for k in order:
         copy = pltpu.make_async_remote_copy(
@@ -109,11 +127,13 @@
     table_in[0] = table_ref[me]
     for copy in tables:
         copy.wait_recv()
-    to_smem = pltpu.make_async_copy(table_in, table_smem, local_sem.at[3])
+    to_smem = pltpu.make_async_copy(table_in, table_smem, local_sem.at[len(pairs)])
     to_smem.start()
     to_smem.wait()
 
     copies = {}
+    loads[1].wait()
+    loads[2].wait()
     for k in order:
         for s in range(slots):
             b = table_smem[k, 0, s]
@@ -144,6 +164,8 @@
         rope_copy.start()
         copies[k] = (lat_copy, rope_copy)
 
+    for at in range(3, 9):
+        loads[at].wait()
     for c in range(2):
         kv[c, pl.ds(0, toks), :] = span_lat[:, c * half : (c + 1) * half]
     kr[pl.ds(0, rope), pl.ds(0, toks)] = span_rope[...]
@@ -156,33 +178,28 @@
     for k in [0] + order:
         kr[pl.ds(rope, 16), pl.ds(base[k], width)] = bias_ref[me ^ k]
 
-    loads[0].wait()
-    loads[1].wait()
     nope32[...] = nope[...].astype(jnp.float32)
     one_col = (lax.broadcasted_iota(jnp.int32, (toks, 128 - rope), 1) == 0).astype(jnp.bfloat16)
     for h in range(heads):
         q_h = nope32[pl.ds(h, toks, stride=heads), :].astype(jnp.bfloat16)
         up = jnp.dot(q_h, key_up[h], preferred_element_type=jnp.float32)
-        q_lat[pl.ds(h * toks, toks), :] = (up * scale).astype(jnp.bfloat16)
+        q_all[pl.ds(h * toks, toks), 0:lat] = (up * scale).astype(jnp.bfloat16)
         rot = rope_q[:, h * rope : (h + 1) * rope].astype(jnp.float32) * scale
-        q_aug[pl.ds(h * toks, toks), :] = jnp.concatenate([rot.astype(jnp.bfloat16), one_col], axis=1)
-
-    tile = 2 * toks
-    tiles = heads // 2
-    nt = (((1,), (1,)), ((), ()))
+        q_all[pl.ds(h * toks, toks), lat:] = jnp.concatenate(
+            [rot.astype(jnp.bfloat16), one_col], axis=1
+        )
+
+    tile = 8 * toks
+    tiles = heads // 8
 
     def attend(start, size, first):
         keys = pl.ds(start, size)
+        for c in range(2):
+            kt[c * half : (c + 1) * half, keys] = kv[c, keys, :].T
 
         def one(t, carry):
             rows = pl.ds(pl.multiple_of(t * tile, tile), tile)
-            s = lax.dot_general(
-                q_lat[rows, 0:half], kv[0, keys, :], nt, preferred_element_type=jnp.float32
-            )
-            s += lax.dot_general(
-                q_lat[rows, half:lat], kv[1, keys, :], nt, preferred_element_type=jnp.float32
-            )
-            s += jnp.dot(q_aug[rows, :], kr[:, keys], preferred_element_type=jnp.float32)
+            s = jnp.dot(q_all[rows, :], kt[:, keys], preferred_element_type=jnp.float32)
             if first:
                 row = lax.broadcasted_iota(jnp.int32, (tile, size), 0) % toks
                 col = lax.broadcasted_iota(jnp.int32, (tile, size), 1)
@@ -203,7 +220,7 @@
                 acc[rows, cols] = mixed if first else acc[rows, cols] * alpha + mixed
             return carry
 
-        lax.fori_loop(0, tiles, one, 0, unroll=2)
+        lax.fori_loop(0, tiles, one, 0)
 
     attend(0, toks + width, True)
 
@@ -243,7 +260,7 @@
         forwards += current
         attend(base[members[0]], len(members) * width, False)
 
-    loads[2].wait()
+    loads[9].wait()
     live = lax.broadcasted_iota(jnp.int32, (toks, value_up.shape[2]), 0) < count_ref[0]
     for h in range(heads):
         rows = pl.ds(h * toks, toks)
@@ -309,41 +326,35 @@
     return pl.pallas_call(
         functools.partial(kernel, sizes),
         out_shape=jax.ShapeDtypeStruct((toks, heads * vdim), jnp.bfloat16),
-        in_specs=[
-            vmem,
-            vmem,
-            pl.BlockSpec(memory_space=pltpu.SMEM),
-            vmem,
-            vmem,
-            vmem,
-            vmem,
-            any_space,
-            vmem,
-            any_space,
-            any_space,
-        ],
+        in_specs=[any_space] * 2 + [pl.BlockSpec(memory_space=pltpu.SMEM)] + [any_space] * 8,
         out_specs=vmem,
         scratch_shapes=[
+            pltpu.VMEM(table.shape, jnp.int32),
+            pltpu.VMEM(bias.shape, jnp.bfloat16),
+            pltpu.VMEM(pool_latent.shape, jnp.bfloat16),
+            pltpu.VMEM(pool_rope.shape, jnp.bfloat16),
+            pltpu.VMEM(span_latent.shape, jnp.bfloat16),
+            pltpu.VMEM(span_rope.shape, jnp.bfloat16),
+            pltpu.VMEM(query_rope.shape, jnp.bfloat16),
             pltpu.VMEM((holders, 8, 128), jnp.int32),
             pltpu.SMEM((holders, 8, 128), jnp.int32),
             pltpu.VMEM((holders, width, lat // 2), jnp.bfloat16),
             pltpu.VMEM((holders, rope // 2, width), jnp.bfloat16),
             pltpu.VMEM((2, keys, lat // 2), jnp.bfloat16),
-            pltpu.VMEM((128, keys), jnp.bfloat16),
+            pltpu.VMEM((lat + 128, keys), jnp.bfloat16),
             pltpu.VMEM((rows, nope_width), jnp.bfloat16),
             pltpu.VMEM((rows, nope_width), jnp.float32),
             pltpu.VMEM(key_up.shape, jnp.bfloat16),
             pltpu.VMEM(value_up.shape, jnp.bfloat16),
-            pltpu.VMEM((rows, lat), jnp.bfloat16),
-            pltpu.VMEM((rows, 128), jnp.bfloat16),
+            pltpu.VMEM((rows, lat + 128), jnp.bfloat16),
             pltpu.VMEM((rows, lat), jnp.float32),
             pltpu.VMEM((rows, 1), jnp.float32),
             pltpu.VMEM((rows, 1), jnp.float32),
-            pltpu.SemaphoreType.DMA((4,)),
+            pltpu.SemaphoreType.DMA((11,)),
         ]
         + [sems] * 10,
         compiler_params=pltpu.CompilerParams(
-            collective_id=0, has_side_effects=True, vmem_limit_bytes=48 * 1024 * 1024
+            collective_id=0, has_side_effects=True, vmem_limit_bytes=56 * 1024 * 1024
         ),
     )(
         table,

time: 85.1 us -> 74.5 us (0.88)
  local copies, waits for them, and re-layouts: 8.12 us -> 2.58 us
  Pallas kernels: 71.6 us -> 66.1 us
    unnamed x16 -> x2, local copies, waits for them, and re-layouts: 8.1 us -> 1.96 us
    pallas_call x1, Pallas kernels: 71.6 us -> 66.1 us  [on_device(): pl.pallas_call(functools.partial(kernel, sizes), out_shape=jax.ShapeDtype...]
where the time goes in v1:
time: 74.5 us; the launch traced here: 73.2 us
  Pallas kernels  66.1 us (89%)
  other arithmetic  3.23 us (4%)
  local copies, waits for them, and re-layouts  2.58 us (3%)
  between operations  1.32 us (2%)
    pallas_call x1, Pallas kernels, on_device(): pl.pallas_call(functools.partial(kernel, sizes), out_shape=jax.ShapeDtype...  66.1 us
    unnamed x2, local copies, waits for them, and re-layouts  1.96 us

profile of v1, /device:TPU:0, one launch (start us, length us, event | category | flops | bytes accessed | tf_op | source)
XLA Modules:
  0.0 73.2 jit_solution(6904888204796115862)
XLA Ops:
  1.3 0.9 %convert_reduce_fusion = s32[24]{0:T(128)S(1)} fusion(s32[24]{0:T(128)} %bitcast.13), kind=kLoop, calls=%fused_computation.6 | loop fusion | flops 2856 | bytes 192 | tf_op jit(solution)/shard_map/reduce_sum | solution.py:306
  2.2 0.7 iota_compare_fusion.1
  2.9 0.8 %fusion.1 = (s32[8,3]{0,1:T(4,128)S(1)}, s32[8,3]{0,1:T(4,128)S(1)}) fusion(s32[24]{0:T(128)S(1)} %subtract_maximum_fusion, pred[3,24]{1,0:T(4,128)(4,1)S(1)} %iota_compare_fusion.2, pred[8,24]{1,0:T(8,128)(4,1)S(1)} %iota_compare_fusion.1, s32[24]{0:T(128)} %bitcast.12), kind=kLoop, calls=%fused_computation.4 | loop fusion | flops 2832 | bytes 648 | tf_op jit(solution)/shard_map/reduce_sum | solution.py:314
  3.7 0.1 fusion.3
  3.8 0.1 copy.14
  3.9 0.6 broadcast_in_dim.65.table_hbm
  4.5 0.7 select_convert_fusion.bias_hbm
  5.2 66.1 %shard_map.118 = bf16[128,2048]{1,0:T(8,128)(2,1)} custom-call(s32[8,8,128]{2,1,0:T(8,128)} %broadcast_in_dim.65.table_hbm, bf16[8,16,384]{2,1,0:T(8,128)(2,1)} %select_convert_fusion.bias_hbm, s32[1]{0:T(128)S(6)} %copy.17.count_ref, bf16[6,128,512]{2,1,0:T(8,128)(2,1)} %pool_lat_hbm.1, bf16[6,64,128]{2,1,0:T(8,128)(2,1)} %pool_rope_hbm.1, ...), custom_call_target="tpu_custom_call" | custom-call | tf_op jit(solution)/shard_map/pallas_call | solution.py:326
  71.4 1.9 %copy.18 = bf16[128,2048]{1,0:T(8,128)(2,1)} copy(bf16[128,2048]{1,0:T(8,128)(2,1)} %shard_map.118) | data formatting | bytes 1048576
  (5 shorter events, 0.0 us)

commit v2 on v1

--- a/solution.py
+++ b/solution.py
@@ -70,8 +70,9 @@
     fwd_lat_recv,
     fwd_rope_send,
     fwd_rope_recv,
+    *line_refs,
 ):
-    holders, slots, heads, toks, block, lat, rope, scale = sizes
+    holders, slots, heads, toks, block, lat, rope, scale, line = sizes
     width = slots * block
     half = lat // 2
     rope_half = rope // 2
@@ -105,64 +106,235 @@
         load.start()
         loads.append(load)
 
-    barrier = pltpu.get_barrier_semaphore()
-    for k in order:
-        pl.semaphore_signal(barrier, inc=1, device_id=peer(k), device_id_type=MESH)
-    pl.semaphore_signal(barrier, inc=1, device_id=sibling, device_id_type=MESH)
-    pl.semaphore_wait(barrier, holders)
-
-    loads[0].wait()
-    tables = []
-    for k in order:
-        copy = pltpu.make_async_remote_copy(
-            src_ref=table_ref.at[me ^ k],
-            dst_ref=table_in.at[k],
-            send_sem=table_send.at[k],
-            recv_sem=table_recv.at[k],
-            device_id=peer(k),
+    if line:
+        z, y = me // 2, me % 2
+        partner = (pool, me ^ 1, core)
+        col_lat, col_rope = line_refs[: line - 1], line_refs[line - 1 : 2 * (line - 1)]
+        (tables_in, tables_smem, own_send, relay_send, col_recv, y_send, y_recv, fwd_send, fwd_recv) = (
+            line_refs[2 * (line - 1) :]
+        )
+        sources = [sorted(range(line), key=lambda s, at=at: (abs(s - at), s)) for at in range(line)]
+        core_cols = pl.ds(pl.multiple_of(core * half, half), half)
+        core_rope = pl.ds(pl.multiple_of(core * rope_half, rope_half), rope_half)
+
+        def source_of(n):
+            code = sum(sources[at][n] << (4 * at) for at in range(line))
+            return (code >> (4 * z)) & 15
+
+        def to_line(at, target, src_lat, src_rope, source, send_sems):
+            n = sources[target].index(source) - 1
+            device = (pool, target * 2 + y, core)
+            return [
+                pltpu.make_async_remote_copy(
+                    src_ref=src,
+                    dst_ref=dst,
+                    send_sem=send_sems.at[part],
+                    recv_sem=col_recv.at[n, part],
+                    device_id=device,
+                    device_id_type=MESH,
+                )
+                for part, (src, dst) in enumerate(
+                    [(src_lat, col_lat[n]), (src_rope, col_rope[n])]
+                )
+            ]
+
+        def own_copies(at):
+            copies = []
+            for side, target in enumerate((at - 1, at + 1)):
+                if 0 <= target < line:
+                    copies += to_line(
+                        at,
+                        target,
+                        pool_lat.at[:, :, core_cols],
+                        pool_rope.at[:, core_rope, :],
+                        at,
+                        own_send.at[side],
+                    )
+            return copies
+
+        def relay_copies(at, n):
+            source = sources[at][n]
+            target = at + 1 if source < at else at - 1
+            if not 0 <= target < line:
+                return []
+            return to_line(
+                at, target, col_lat[n - 1], col_rope[n - 1], source, relay_send.at[n - 1]
+            )
+
+        def arrive(at, n):
+            for part, buf in enumerate((col_lat[n - 1], col_rope[n - 1])):
+                pltpu.make_async_copy(buf, buf, col_recv.at[n - 1, part]).wait()
+            for copy in relay_copies(at, n):
+                copy.start()
+
+        def each_place(body):
+            for at in range(line):
+                pl.when(z == at)(functools.partial(body, at))
+
+        def greet(at):
+            near = [t for t in (at - 1, at + 1) if 0 <= t < line]
+            for t in near:
+                pl.semaphore_signal(
+                    barrier, inc=1, device_id=(pool, t * 2 + y, core), device_id_type=MESH
+                )
+            pl.semaphore_wait(barrier, len(near) + 2)
+
+        barrier = pltpu.get_barrier_semaphore()
+        pl.semaphore_signal(barrier, inc=1, device_id=partner, device_id_type=MESH)
+        pl.semaphore_signal(barrier, inc=1, device_id=sibling, device_id_type=MESH)
+        each_place(greet)
+        loads[0].wait()
+        table_copy = pltpu.make_async_remote_copy(
+            src_ref=table_ref,
+            dst_ref=tables_in,
+            send_sem=table_send.at[0],
+            recv_sem=table_recv.at[0],
+            device_id=partner,
             device_id_type=MESH,
         )
-        copy.start()
-        tables.append(copy)
-    table_in[0] = table_ref[me]
-    for copy in tables:
-        copy.wait_recv()
-    to_smem = pltpu.make_async_copy(table_in, table_smem, local_sem.at[len(pairs)])
-    to_smem.start()
-    to_smem.wait()
-
-    copies = {}
-    loads[1].wait()
-    loads[2].wait()
-    for k in order:
-        for s in range(slots):
-            b = table_smem[k, 0, s]
-            rows = pl.ds(s * block, block)
-            send_lat[k, rows, :] = pool_lat[b, :, pl.ds(pl.multiple_of(core * half, half), half)]
-            send_rope[k, :, rows] = pool_rope[
-                b, pl.ds(pl.multiple_of(core * rope_half, rope_half), rope_half), :
+        table_copy.start()
+        own_table = pltpu.make_async_copy(table_ref, table_smem, local_sem.at[len(pairs)])
+        own_table.start()
+        loads[1].wait()
+        loads[2].wait()
+
+        def send_own(at):
+            for copy in own_copies(at):
+                copy.start()
+
+        each_place(send_own)
+        own_table.wait()
+        table_copy.wait_recv()
+        partner_table = pltpu.make_async_copy(tables_in, tables_smem, local_sem.at[len(pairs)])
+        partner_table.start()
+        partner_table.wait()
+        own_base = [toks + 2 * n * width for n in range(line)]
+        y_base = [toks + (2 * n + 1) * width for n in range(line)]
+
+        def y_copies(n):
+            return [
+                pltpu.make_async_remote_copy(
+                    src_ref=src,
+                    dst_ref=dst,
+                    send_sem=y_send.at[n, part],
+                    recv_sem=y_recv.at[n, part],
+                    device_id=partner,
+                    device_id_type=MESH,
+                )
+                for part, (src, dst) in enumerate(
+                    [
+                        (send_lat.at[n], kv.at[core, pl.ds(y_base[n], width), :]),
+                        (send_rope.at[n], kr.at[core_rope, pl.ds(y_base[n], width)]),
+                    ]
+                )
             ]
-        lat_copy = pltpu.make_async_remote_copy(
-            src_ref=send_lat.at[k],
-            dst_ref=kv.at[core, pl.ds(base[k], width), :],
-            send_sem=lat_send.at[k],
-            recv_sem=lat_recv.at[k],
-            device_id=peer(k),
-            device_id_type=MESH,
-        )
-        rope_copy = pltpu.make_async_remote_copy(
-            src_ref=send_rope.at[k],
-            dst_ref=kr.at[
-                pl.ds(pl.multiple_of(core * rope_half, rope_half), rope_half), pl.ds(base[k], width)
-            ],
-            send_sem=rope_send.at[k],
-            recv_sem=rope_recv.at[k],
-            device_id=peer(k),
-            device_id_type=MESH,
-        )
-        lat_copy.start()
-        rope_copy.start()
-        copies[k] = (lat_copy, rope_copy)
+
+        def pack_y(n):
+            holder = source_of(n) * 2 + y
+            for s in range(slots):
+                b = tables_smem[holder, 0, s]
+                rows = pl.ds(s * block, block)
+                if n == 0:
+                    send_lat[n, rows, :] = pool_lat[b, :, core_cols]
+                    send_rope[n, :, rows] = pool_rope[b, core_rope, :]
+                else:
+                    send_lat[n, rows, :] = col_lat[n - 1][b]
+                    send_rope[n, :, rows] = col_rope[n - 1][b]
+            for copy in y_copies(n):
+                copy.start()
+
+        def sibling_copies(n, kind, start):
+            lat_rows = kv.at[core, pl.ds(start, width), :]
+            rope_rows = kr.at[core_rope, pl.ds(start, width)]
+            return [
+                pltpu.make_async_remote_copy(
+                    src_ref=ref,
+                    dst_ref=ref,
+                    send_sem=fwd_send.at[n, kind, part],
+                    recv_sem=fwd_recv.at[n, kind, part],
+                    device_id=sibling,
+                    device_id_type=MESH,
+                )
+                for part, ref in enumerate([lat_rows, rope_rows])
+            ]
+
+        def pack_own(n):
+            holder = source_of(n) * 2 + y
+            for s in range(slots):
+                b = table_smem[holder, 0, s]
+                rows = pl.ds(own_base[n] + s * block, block)
+                kv[core, rows, :] = col_lat[n - 1][b]
+                kr[core_rope, rows] = col_rope[n - 1][b]
+            copies = sibling_copies(n, 0, own_base[n])
+            for copy in copies:
+                copy.start()
+            return copies
+
+        pack_y(0)
+        own_row = me
+        places = [(own_base[n], source_of(n) * 2 + y) for n in range(line)]
+        places += [(y_base[n], source_of(n) * 2 + 1 - y) for n in range(line)]
+    else:
+        barrier = pltpu.get_barrier_semaphore()
+        for k in order:
+            pl.semaphore_signal(barrier, inc=1, device_id=peer(k), device_id_type=MESH)
+        pl.semaphore_signal(barrier, inc=1, device_id=sibling, device_id_type=MESH)
+        pl.semaphore_wait(barrier, holders)
+
+        loads[0].wait()
+        tables = []
+        for k in order:
+            copy = pltpu.make_async_remote_copy(
+                src_ref=table_ref.at[me ^ k],
+                dst_ref=table_in.at[k],
+                send_sem=table_send.at[k],
+                recv_sem=table_recv.at[k],
+                device_id=peer(k),
+                device_id_type=MESH,
+            )
+            copy.start()
+            tables.append(copy)
+        table_in[0] = table_ref[me]
+        for copy in tables:
+            copy.wait_recv()
+        to_smem = pltpu.make_async_copy(table_in, table_smem, local_sem.at[len(pairs)])
+        to_smem.start()
+        to_smem.wait()
+
+        copies = {}
+        loads[1].wait()
+        loads[2].wait()
+        for k in order:
+            for s in range(slots):
+                b = table_smem[k, 0, s]
+                rows = pl.ds(s * block, block)
+                send_lat[k, rows, :] = pool_lat[b, :, pl.ds(pl.multiple_of(core * half, half), half)]
+                send_rope[k, :, rows] = pool_rope[
+                    b, pl.ds(pl.multiple_of(core * rope_half, rope_half), rope_half), :
+                ]
+            lat_copy = pltpu.make_async_remote_copy(
+                src_ref=send_lat.at[k],
+                dst_ref=kv.at[core, pl.ds(base[k], width), :],
+                send_sem=lat_send.at[k],
+                recv_sem=lat_recv.at[k],
+                device_id=peer(k),
+                device_id_type=MESH,
+            )
+            rope_copy = pltpu.make_async_remote_copy(
+                src_ref=send_rope.at[k],
+                dst_ref=kr.at[
+                    pl.ds(pl.multiple_of(core * rope_half, rope_half), rope_half), pl.ds(base[k], width)
+                ],
+                send_sem=rope_send.at[k],
+                recv_sem=rope_recv.at[k],
+                device_id=peer(k),
+                device_id_type=MESH,
+            )
+            lat_copy.start()
+            rope_copy.start()
+            copies[k] = (lat_copy, rope_copy)
+        own_row = 0
+        places = [(base[k], me ^ k) for k in [0] + order]
 
     for at in range(3, 9):
         loads[at].wait()
@@ -171,12 +343,12 @@
     kr[pl.ds(0, rope), pl.ds(0, toks)] = span_rope[...]
     kr[pl.ds(rope, 128 - rope), :] = jnp.zeros((128 - rope, kr.shape[1]), jnp.bfloat16)
     for s in range(slots):
-        b = table_smem[0, 0, s]
+        b = table_smem[own_row, 0, s]
         for c in range(2):
             kv[c, pl.ds(toks + s * block, block), :] = pool_lat[b, :, c * half : (c + 1) * half]
         kr[pl.ds(0, rope), pl.ds(toks + s * block, block)] = pool_rope[b]
-    for k in [0] + order:
-        kr[pl.ds(rope, 16), pl.ds(base[k], width)] = bias_ref[me ^ k]
+    for start, holder in places:
+        kr[pl.ds(rope, 16), pl.ds(start, width)] = bias_ref[holder]
 
     nope32[...] = nope[...].astype(jnp.float32)
     one_col = (lax.broadcasted_iota(jnp.int32, (toks, 128 - rope), 1) == 0).astype(jnp.bfloat16)
@@ -224,41 +396,74 @@
 
     attend(0, toks + width, True)
 
-    forwards = []
-    group = max(1, 768 // width)
-    for at in range(0, len(order), group):
-        members = order[at : at + group]
-        current = []
-        for k in members:
-            copies[k][0].wait_recv()
-            copies[k][1].wait_recv()
-            lat_rows = kv.at[core, pl.ds(base[k], width), :]
-            rope_rows = kr.at[
-                pl.ds(pl.multiple_of(core * rope_half, rope_half), rope_half), pl.ds(base[k], width)
-            ]
-            lat_fwd = pltpu.make_async_remote_copy(
-                src_ref=lat_rows,
-                dst_ref=lat_rows,
-                send_sem=fwd_lat_send.at[k],
-                recv_sem=fwd_lat_recv.at[k],
-                device_id=sibling,
-                device_id_type=MESH,
-            )
-            rope_fwd = pltpu.make_async_remote_copy(
-                src_ref=rope_rows,
-                dst_ref=rope_rows,
-                send_sem=fwd_rope_send.at[k],
-                recv_sem=fwd_rope_recv.at[k],
-                device_id=sibling,
-                device_id_type=MESH,
-            )
-            lat_fwd.start()
-            rope_fwd.start()
-            current += [lat_fwd, rope_fwd]
+    if line:
+        forwards = []
+
+        def take_y(n):
+            for copy in y_copies(n):
+                copy.wait_recv()
+            copies = sibling_copies(n, 1, y_base[n])
+            for copy in copies:
+                copy.start()
+            return copies
+
+        for n in range(1, line):
+
+            def arrivals(at, n=n):
+                inner = 0 < at < line - 1
+                ahead = [n] if not inner else [1, 2] if n == 1 else [n + 1]
+                for m in ahead:
+                    if m < line:
+                        arrive(at, m)
+
+            each_place(arrivals)
+            pack_y(n)
+            current = pack_own(n) + take_y(n - 1)
+            for copy in current:
+                copy.wait_recv()
+            forwards += current
+            attend(y_base[n - 1], 2 * width, False)
+        current = take_y(line - 1)
         for copy in current:
             copy.wait_recv()
         forwards += current
-        attend(base[members[0]], len(members) * width, False)
+        attend(y_base[line - 1], width, False)
+    else:
+        forwards = []
+        group = max(1, 768 // width)
+        for at in range(0, len(order), group):
+            members = order[at : at + group]
+            current = []
+            for k in members:
+                copies[k][0].wait_recv()
+                copies[k][1].wait_recv()
+                lat_rows = kv.at[core, pl.ds(base[k], width), :]
+                rope_rows = kr.at[
+                    pl.ds(pl.multiple_of(core * rope_half, rope_half), rope_half), pl.ds(base[k], width)
+                ]
+                lat_fwd = pltpu.make_async_remote_copy(
+                    src_ref=lat_rows,
+                    dst_ref=lat_rows,
+                    send_sem=fwd_lat_send.at[k],
+                    recv_sem=fwd_lat_recv.at[k],
+                    device_id=sibling,
+                    device_id_type=MESH,
+                )
+                rope_fwd = pltpu.make_async_remote_copy(
+                    src_ref=rope_rows,
+                    dst_ref=rope_rows,
+                    send_sem=fwd_rope_send.at[k],
+                    recv_sem=fwd_rope_recv.at[k],
+                    device_id=sibling,
+                    device_id_type=MESH,
+                )
+                lat_fwd.start()
+                rope_fwd.start()
+                current += [lat_fwd, rope_fwd]
+            for copy in current:
+                copy.wait_recv()
+            forwards += current
+            attend(base[members[0]], len(members) * width, False)
 
     loads[9].wait()
     live = lax.broadcasted_iota(jnp.int32, (toks, value_up.shape[2]), 0) < count_ref[0]
@@ -269,11 +474,28 @@
         vdim = value_up.shape[2]
         out_ref[:, h * vdim : (h + 1) * vdim] = jnp.where(live, up, 0.0).astype(out_ref.dtype)
 
-    for copy in tables + forwards:
-        copy.wait_send()
-    for k in order:
-        copies[k][0].wait_send()
-        copies[k][1].wait_send()
+    if line:
+
+        def drain(at):
+            for copy in own_copies(at):
+                copy.wait_send()
+            for n in range(1, line):
+                for copy in relay_copies(at, n):
+                    copy.wait_send()
+
+        each_place(drain)
+        table_copy.wait_send()
+        for n in range(line):
+            for copy in y_copies(n):
+                copy.wait_send()
+        for copy in forwards:
+            copy.wait_send()
+    else:
+        for copy in tables + forwards:
+            copy.wait_send()
+        for k in order:
+            copies[k][0].wait_send()
+            copies[k][1].wait_send()
 
 
 def on_device(
@@ -322,7 +544,24 @@
     vmem = pl.BlockSpec(memory_space=pltpu.VMEM)
     any_space = pl.BlockSpec(memory_space=pl.ANY)
     sems = pltpu.SemaphoreType.DMA((holders,))
-    sizes = (holders, slots, heads, toks, block, lat, rope, scale)
+    line = holders // 2 if holders <= 8 else 0
+    line_scratch = []
+    if line:
+        stored = pool_latent.shape[0]
+        line_scratch = [pltpu.VMEM((stored, block, lat // 2), jnp.bfloat16)] * (line - 1)
+        line_scratch += [pltpu.VMEM((stored, rope // 2, block), jnp.bfloat16)] * (line - 1)
+        line_scratch += [
+            pltpu.VMEM(table.shape, jnp.int32),
+            pltpu.SMEM(table.shape, jnp.int32),
+            pltpu.SemaphoreType.DMA((2, 2)),
+            pltpu.SemaphoreType.DMA((line, 2)),
+            pltpu.SemaphoreType.DMA((line, 2)),
+            pltpu.SemaphoreType.DMA((line, 2)),
+            pltpu.SemaphoreType.DMA((line, 2)),
+            pltpu.SemaphoreType.DMA((line, 2, 2)),
+            pltpu.SemaphoreType.DMA((line, 2, 2)),
+        ]
+    sizes = (holders, slots, heads, toks, block, lat, rope, scale, line)
     return pl.pallas_call(
         functools.partial(kernel, sizes),
         out_shape=jax.ShapeDtypeStruct((toks, heads * vdim), jnp.bfloat16),
@@ -352,7 +591,8 @@
             pltpu.VMEM((rows, 1), jnp.float32),
             pltpu.SemaphoreType.DMA((11,)),
         ]
-        + [sems] * 10,
+        + [sems] * 10
+        + line_scratch,
         compiler_params=pltpu.CompilerParams(
             collective_id=0, has_side_effects=True, vmem_limit_bytes=56 * 1024 * 1024
         ),

time: 74.5 us -> 60.5 us (0.81); the launches traced: 73.2 us -> 60.3 us
  Pallas kernels: 66.1 us -> 53.2 us
    pallas_call x1, Pallas kernels: 66.1 us -> 53.2 us  [on_device(): pl.pallas_call(functools.partial(kernel, sizes), out_shape=jax.ShapeDtype...]
where the time goes in v2:
time: 60.5 us; the launch traced here: 60.3 us
  Pallas kernels  53.2 us (88%)
  other arithmetic  3.23 us (5%)
  local copies, waits for them, and re-layouts  2.58 us (4%)
  between operations  1.32 us (2%)
    pallas_call x1, Pallas kernels, on_device(): pl.pallas_call(functools.partial(kernel, sizes), out_shape=jax.ShapeDtype...  53.2 us
    unnamed x2, local copies, waits for them, and re-layouts  1.96 us

profile of v2, /device:TPU:0, one launch (start us, length us, event | category | flops | bytes accessed | tf_op | source)
XLA Modules:
  0.0 60.3 jit_solution(6867725983325927833)
XLA Ops:
  1.3 0.9 %convert_reduce_fusion = s32[24]{0:T(128)S(1)} fusion(s32[24]{0:T(128)} %bitcast.13), kind=kLoop, calls=%fused_computation.6 | loop fusion | flops 2856 | bytes 192 | tf_op jit(solution)/shard_map/reduce_sum | solution.py:528
  2.2 0.7 %iota_compare_fusion.1 = pred[8,24]{1,0:T(8,128)(4,1)S(1)} fusion(s32[24]{0:T(128)} %bitcast.14), kind=kLoop, calls=%fused_computation.10 | loop fusion | flops 192 | bytes 288 | tf_op jit(solution)/shard_map/eq | solution.py:529
  2.9 0.8 %fusion.1 = (s32[8,3]{0,1:T(4,128)S(1)}, s32[8,3]{0,1:T(4,128)S(1)}) fusion(s32[24]{0:T(128)S(1)} %subtract_maximum_fusion, pred[3,24]{1,0:T(4,128)(4,1)S(1)} %iota_compare_fusion.2, pred[8,24]{1,0:T(8,128)(4,1)S(1)} %iota_compare_fusion.1, s32[24]{0:T(128)} %bitcast.12), kind=kLoop, calls=%fused_computation.4 | loop fusion | flops 2832 | bytes 648 | tf_op jit(solution)/shard_map/reduce_sum | solution.py:536
  3.7 0.1 fusion.3
  3.8 0.1 copy.14
  3.9 0.6 %broadcast_in_dim.65.table_hbm = s32[8,8,128]{2,1,0:T(8,128)} broadcast(s32[8,128]{1,0:T(8,128)S(1)} %pad.4.clone), dimensions={0,2} | broadcast | bytes 36864 | tf_op jit(solution)/shard_map/broadcast_in_dim | solution.py:533
  4.5 0.7 %select_convert_fusion.bias_hbm = bf16[8,16,384]{2,1,0:T(8,128)(2,1)} fusion(bf16[8,384]{1,0:T(8,128)(2,1)S(1)} %fusion.3, pred[16]{0:T(512)(128)(4,1)S(1)} %iota_compare_fusion.3), kind=kLoop, calls=%fused_computation | loop fusion | flops 49152 | bytes 104464 | tf_op jit(solution)/shard_map/convert_element_type | solution.py:540
  5.2 53.2 %shard_map.118 = bf16[128,2048]{1,0:T(8,128)(2,1)} custom-call(s32[8,8,128]{2,1,0:T(8,128)} %broadcast_in_dim.65.table_hbm, bf16[8,16,384]{2,1,0:T(8,128)(2,1)} %select_convert_fusion.bias_hbm, s32[1]{0:T(128)S(6)} %copy.17.count_ref, bf16[6,128,512]{2,1,0:T(8,128)(2,1)} %pool_lat_hbm.1, bf16[6,64,128]{2,1,0:T(8,128)(2,1)} %pool_rope_hbm.1, ...), custom_call_target="tpu_custom_call" | custom-call | tf_op jit(solution)/shard_map/pallas_call | solution.py:565
  58.4 1.9 %copy.18 = bf16[128,2048]{1,0:T(8,128)(2,1)} copy(bf16[128,2048]{1,0:T(8,128)(2,1)} %shard_map.118) | data formatting | bytes 1048576
  (5 shorter events, 0.0 us)

commit v3 on v2

--- a/solution.py
+++ b/solution.py
@@ -26,9 +26,11 @@
 
 def kernel(
     sizes,
-    table_hbm,
-    bias_hbm,
+    hit_scalars,
+    prefix_ref,
     count_ref,
+    holders_hbm,
+    blocks_hbm,
     pool_lat_hbm,
     pool_rope_hbm,
     span_lat_hbm,
@@ -40,6 +42,8 @@
     out_ref,
     table_ref,
     bias_ref,
+    holders_ref,
+    blocks_ref,
     pool_lat,
     pool_rope,
     span_lat,
@@ -89,22 +93,45 @@
         return (pool, me ^ k, core)
 
     pairs = [
-        (table_hbm, table_ref),
         (pool_lat_hbm, pool_lat),
         (pool_rope_hbm, pool_rope),
         (span_lat_hbm, span_lat),
         (span_rope_hbm, span_rope),
-        (bias_hbm, bias_ref),
         (nope_hbm, nope),
         (key_up_hbm, key_up),
         (rope_q_hbm, rope_q),
         (value_up_hbm, value_up),
+        (holders_hbm, holders_ref),
+        (blocks_hbm, blocks_ref),
     ]
     loads = []
     for at, (src, dst) in enumerate(pairs):
         load = pltpu.make_async_copy(src, dst, local_sem.at[at])
         load.start()
         loads.append(load)
+
+    def make_tables():
+        loads[8].wait()
+        loads[9].wait()
+        list_len = holders_ref.shape[1]
+        hit_row, block_row = holders_ref[...], blocks_ref[...]
+        entry = lax.broadcasted_iota(jnp.int32, (1, list_len), 1)
+        rank = jnp.zeros((1, list_len), jnp.int32)
+        for j in range(list_len):
+            rank += jnp.where((hit_row == hit_scalars[0, j]) & (entry > j), 1, 0)
+        left = jnp.maximum(prefix_ref[0] - entry * block, 0)
+        holder = lax.broadcasted_iota(jnp.int32, (holders, list_len), 0)
+        place = lax.broadcasted_iota(jnp.int32, (holders, 128), 1)
+        token = lax.broadcasted_iota(jnp.int32, (holders, block), 1)
+        ids = jnp.zeros((holders, 128), jnp.int32)
+        for s in range(slots):
+            match = (hit_row == holder) & (rank == s)
+            picked = jnp.sum(jnp.where(match, block_row, 0), axis=1, keepdims=True)
+            seen = jnp.sum(jnp.where(match, left, 0), axis=1, keepdims=True)
+            ids = jnp.where(place == s, picked, ids)
+            bias_ref[:, s * block : (s + 1) * block] = jnp.where(token >= seen, MASKED, 0.0)
+        for h in range(holders):
+            table_ref[h] = jnp.broadcast_to(ids[h : h + 1, :], (8, 128))
 
     if line:
         z, y = me // 2, me % 2
@@ -182,8 +209,8 @@
         barrier = pltpu.get_barrier_semaphore()
         pl.semaphore_signal(barrier, inc=1, device_id=partner, device_id_type=MESH)
         pl.semaphore_signal(barrier, inc=1, device_id=sibling, device_id_type=MESH)
+        make_tables()
         each_place(greet)
-        loads[0].wait()
         table_copy = pltpu.make_async_remote_copy(
             src_ref=table_ref,
             dst_ref=tables_in,
@@ -195,8 +222,8 @@
         table_copy.start()
         own_table = pltpu.make_async_copy(table_ref, table_smem, local_sem.at[len(pairs)])
         own_table.start()
+        loads[0].wait()
         loads[1].wait()
-        loads[2].wait()
 
         def send_own(at):
             for copy in own_copies(at):
@@ -279,9 +306,9 @@
         for k in order:
             pl.semaphore_signal(barrier, inc=1, device_id=peer(k), device_id_type=MESH)
         pl.semaphore_signal(barrier, inc=1, device_id=sibling, device_id_type=MESH)
+        make_tables()
         pl.semaphore_wait(barrier, holders)
 
-        loads[0].wait()
         tables = []
         for k in order:
             copy = pltpu.make_async_remote_copy(
@@ -302,8 +329,8 @@
         to_smem.wait()
 
         copies = {}
+        loads[0].wait()
         loads[1].wait()
-        loads[2].wait()
         for k in order:
             for s in range(slots):
                 b = table_smem[k, 0, s]
@@ -336,7 +363,7 @@
         own_row = 0
         places = [(base[k], me ^ k) for k in [0] + order]
 
-    for at in range(3, 9):
+    for at in range(2, 7):
         loads[at].wait()
     for c in range(2):
         kv[c, pl.ds(0, toks), :] = span_lat[:, c * half : (c + 1) * half]
@@ -347,8 +374,10 @@
         for c in range(2):
             kv[c, pl.ds(toks + s * block, block), :] = pool_lat[b, :, c * half : (c + 1) * half]
         kr[pl.ds(0, rope), pl.ds(toks + s * block, block)] = pool_rope[b]
+    top_row = lax.broadcasted_iota(jnp.int32, (16, width), 0) == 0
     for start, holder in places:
-        kr[pl.ds(rope, 16), pl.ds(start, width)] = bias_ref[holder]
+        row = bias_ref[pl.ds(holder, 1), :]
+        kr[pl.ds(rope, 16), pl.ds(start, width)] = jnp.where(top_row, row, 0.0).astype(jnp.bfloat16)
 
     nope32[...] = nope[...].astype(jnp.float32)
     one_col = (lax.broadcasted_iota(jnp.int32, (toks, 128 - rope), 1) == 0).astype(jnp.bfloat16)
@@ -361,8 +390,9 @@
             [rot.astype(jnp.bfloat16), one_col], axis=1
         )
 
-    tile = 8 * toks
-    tiles = heads // 8
+    tile = 16 * toks
+    part = 2 * toks
+    tiles = heads // 16
 
     def attend(start, size, first):
         keys = pl.ds(start, size)
@@ -370,26 +400,44 @@
             kt[c * half : (c + 1) * half, keys] = kv[c, keys, :].T
 
         def one(t, carry):
-            rows = pl.ds(pl.multiple_of(t * tile, tile), tile)
-            s = jnp.dot(q_all[rows, :], kt[:, keys], preferred_element_type=jnp.float32)
+            parts = [
+                pl.ds(pl.multiple_of(t * tile + at * part, part), part) for at in range(tile // part)
+            ]
+            scores = [
+                jnp.dot(q_all[rows, :], kt[:, keys], preferred_element_type=jnp.float32)
+                for rows in parts
+            ]
             if first:
-                row = lax.broadcasted_iota(jnp.int32, (tile, size), 0) % toks
-                col = lax.broadcasted_iota(jnp.int32, (tile, size), 1)
-                s = jnp.where((col <= row) | (col >= toks), s, MASKED)
-            top = jnp.max(s, axis=1, keepdims=True)
-            if not first:
-                old = peak[rows, :]
-                top = jnp.maximum(top, old)
-                alpha = jnp.exp2(old - top)
-            p = jnp.exp2(s - top)
-            summed = jnp.sum(p, axis=1, keepdims=True)
-            p = p.astype(jnp.bfloat16)
-            peak[rows, :] = top
-            total[rows, :] = summed if first else total[rows, :] * alpha + summed
-            for c in range(2):
-                cols = pl.ds(c * half, half)
-                mixed = jnp.dot(p, kv[c, keys, :], preferred_element_type=jnp.float32)
-                acc[rows, cols] = mixed if first else acc[rows, cols] * alpha + mixed
+                row = lax.broadcasted_iota(jnp.int32, (part, size), 0) % toks
+                col = lax.broadcasted_iota(jnp.int32, (part, size), 1)
+                seen = (col <= row) | (col >= toks)
+                scores = [jnp.where(seen, s, MASKED) for s in scores]
+            else:
+                old = [peak[rows, :] for rows in parts]
+                old_total = [total[rows, :] for rows in parts]
+            tops, probs, sums, alphas = [], [], [], []
+            for at, s in enumerate(scores):
+                top = jnp.max(s, axis=1, keepdims=True)
+                if not first:
+                    top = jnp.maximum(top, old[at])
+                    alphas.append(jnp.exp2(old[at] - top))
+                p = jnp.exp2(s - top)
+                tops.append(top)
+                sums.append(jnp.sum(p, axis=1, keepdims=True))
+                probs.append(p.astype(jnp.bfloat16))
+            mixed = [
+                [jnp.dot(p, kv[c, keys, :], preferred_element_type=jnp.float32) for c in range(2)]
+                for p in probs
+            ]
+            for at, rows in enumerate(parts):
+                peak[rows, :] = tops[at]
+                total[rows, :] = sums[at] if first else old_total[at] * alphas[at] + sums[at]
+                for c in range(2):
+                    cols = pl.ds(c * half, half)
+                    if first:
+                        acc[rows, cols] = mixed[at][c]
+                    else:
+                        acc[rows, cols] = acc[rows, cols] * alphas[at] + mixed[at][c]
             return carry
 
         lax.fori_loop(0, tiles, one, 0)
@@ -465,11 +513,11 @@
             forwards += current
             attend(base[members[0]], len(members) * width, False)
 
-    loads[9].wait()
+    loads[7].wait()
     live = lax.broadcasted_iota(jnp.int32, (toks, value_up.shape[2]), 0) < count_ref[0]
     for h in range(heads):
         rows = pl.ds(h * toks, toks)
-        mixed = (acc[rows, :] / total[rows, :]).astype(jnp.bfloat16)
+        mixed = (acc[rows, :] * (1.0 / total[rows, :])).astype(jnp.bfloat16)
         up = jnp.dot(mixed, value_up[h], preferred_element_type=jnp.float32)
         vdim = value_up.shape[2]
         out_ref[:, h * vdim : (h + 1) * vdim] = jnp.where(live, up, 0.0).astype(out_ref.dtype)
@@ -523,22 +571,6 @@
     width = slots * block
     scale = float(nope_width + rope) ** (-0.5) * math.log2(math.e)
 
-    row = hit_holders[0]
-    entry = jnp.arange(list_len)
-    rank = jnp.sum((row[:, None] == row[None, :]) & (entry[None, :] < entry[:, None]), axis=1)
-    match = (row[None, None, :] == jnp.arange(holders)[:, None, None]) & (
-        rank[None, None, :] == jnp.arange(slots)[None, :, None]
-    )
-    ids = jnp.sum(jnp.where(match, hit_blocks[0][None, None, :], 0), axis=2)
-    table = jnp.broadcast_to(
-        jnp.pad(ids, ((0, 0), (0, 128 - slots)))[:, None, :], (holders, 8, 128)
-    ).astype(jnp.int32)
-    seen = jnp.sum(jnp.where(match, jnp.maximum(prefix_len[0] - entry * block, 0), 0), axis=2)
-    hidden = jnp.arange(block)[None, None, :] >= seen[:, :, None]
-    bias = jnp.where(hidden, MASKED, 0.0).reshape(holders, 1, width)
-    first_row = jnp.arange(16)[None, :, None] == 0
-    bias = jnp.where(first_row, bias, 0.0).astype(jnp.bfloat16)
-
     keys = toks + holders * width
     rows = heads * toks
     vmem = pl.BlockSpec(memory_space=pltpu.VMEM)
@@ -551,8 +583,8 @@
         line_scratch = [pltpu.VMEM((stored, block, lat // 2), jnp.bfloat16)] * (line - 1)
         line_scratch += [pltpu.VMEM((stored, rope // 2, block), jnp.bfloat16)] * (line - 1)
         line_scratch += [
-            pltpu.VMEM(table.shape, jnp.int32),
-            pltpu.SMEM(table.shape, jnp.int32),
+            pltpu.VMEM((holders, 8, 128), jnp.int32),
+            pltpu.SMEM((holders, 8, 128), jnp.int32),
             pltpu.SemaphoreType.DMA((2, 2)),
             pltpu.SemaphoreType.DMA((line, 2)),
             pltpu.SemaphoreType.DMA((line, 2)),
@@ -565,11 +597,13 @@
     return pl.pallas_call(
         functools.partial(kernel, sizes),
         out_shape=jax.ShapeDtypeStruct((toks, heads * vdim), jnp.bfloat16),
-        in_specs=[any_space] * 2 + [pl.BlockSpec(memory_space=pltpu.SMEM)] + [any_space] * 8,
+        in_specs=[pl.BlockSpec(memory_space=pltpu.SMEM)] * 3 + [any_space] * 10,
         out_specs=vmem,
         scratch_shapes=[
-            pltpu.VMEM(table.shape, jnp.int32),
-            pltpu.VMEM(bias.shape, jnp.bfloat16),
+            pltpu.VMEM((holders, 8, 128), jnp.int32),
+            pltpu.VMEM((holders, width), jnp.float32),
+            pltpu.VMEM(hit_holders.shape, jnp.int32),
+            pltpu.VMEM(hit_blocks.shape, jnp.int32),
             pltpu.VMEM(pool_latent.shape, jnp.bfloat16),
             pltpu.VMEM(pool_rope.shape, jnp.bfloat16),
             pltpu.VMEM(span_latent.shape, jnp.bfloat16),
@@ -597,9 +631,11 @@
             collective_id=0, has_side_effects=True, vmem_limit_bytes=56 * 1024 * 1024
         ),
     )(
-        table,
-        bias,
+        hit_holders,
+        prefix_len,
         span_len,
+        hit_holders,
+        hit_blocks,
         pool_latent,
         pool_rope,
         span_latent,

time: 60.5 us -> 54.8 us (0.906)
  other arithmetic: 3.23 us -> 0 us
  Pallas kernels: 53.2 us -> 51.4 us
  local copies, waits for them, and re-layouts: 2.58 us -> 1.88 us
    reduce_sum x2 -> x0, other arithmetic: 1.75 us -> none  [the longest x1 0.91 us: on_device(): jnp.sum((row[:, None] == row[None, :]) & (entry[None, :] < entry[:, None]...]
    pallas_call x1, Pallas kernels: 53.2 us -> 51.4 us  [on_device(): pl.pallas_call(functools.partial(kernel, sizes), out_shape=jax.ShapeDtype...]
    convert_element_type x1 -> x0, other arithmetic: 0.72 us -> none  [on_device(): bias = jnp.where(first_row, bias, 0.0).astype(jnp.bfloat16)]
    eq x3 -> x0, other arithmetic: 0.68 us -> none  [the longest x1 0.66 us: on_device(): row[None, None, :] == jnp.arange(holders)[:, None, None]]
    broadcast_in_dim x1 -> x0, local copies, waits for them, and re-layouts: 0.61 us -> none  [on_device(): jnp.broadcast_to(jnp.pad(ids, ((0, 0), (0, 128 - slots)))[:, None, :], (h...]
    unnamed x2 -> x1, local copies, waits for them, and re-layouts: 1.96 us -> 1.88 us
where the time goes in v3:
time: 54.8 us; the launch traced here: 54.6 us
  Pallas kernels  51.4 us (94%)
  local copies, waits for them, and re-layouts  1.88 us (3%)
  between operations  1.31 us (2%)
    pallas_call x1, Pallas kernels, on_device(): pl.pallas_call(functools.partial(kernel, sizes), out_shape=jax.ShapeDtype...  51.4 us
    unnamed x1, local copies, waits for them, and re-layouts  1.88 us

profile of v3, /device:TPU:0, one launch (start us, length us, event | category | flops | bytes accessed | tf_op | source)
XLA Modules:
  0.0 54.6 jit_solution(10243551798434181622)
XLA Ops:
  1.3 51.4 %shard_map.118 = bf16[128,2048]{1,0:T(8,128)(2,1)} custom-call(s32[1,24]{1,0:T(1,128)} %holders_hbm.1, s32[1]{0:T(128)S(6)} %copy.14.prefix_ref, s32[1]{0:T(128)S(6)} %copy.15.count_ref, s32[1,24]{1,0:T(1,128)} %holders_hbm.1, s32[1,24]{1,0:T(1,128)} %blocks_hbm.1, bf16[6,128,512]{2,1,0:T(8,128)(2,1)} %pool_lat_hbm.1, bf16[6,64,128]{2,1,0:T(8,128)(2,1)} %pool_rope_hbm.1, ...), custom_call_target="tpu_custom_call" | custom-call | tf_op jit(solution)/shard_map/pallas_call | solution.py:597
  52.7 1.9 %copy.16 = bf16[128,2048]{1,0:T(8,128)(2,1)} copy(bf16[128,2048]{1,0:T(8,128)(2,1)} %shard_map.118) | data formatting | bytes 1048576

commit v4 on v3

--- a/solution.py
+++ b/solution.py
@@ -464,9 +464,10 @@
                     if m < line:
                         arrive(at, m)
 
+            current = take_y(n - 1)
             each_place(arrivals)
             pack_y(n)
-            current = pack_own(n) + take_y(n - 1)
+            current += pack_own(n)
             for copy in current:
                 copy.wait_recv()
             forwards += current

time: 54.8 us -> 54.5 us (level)
  no operation moved by 1% of the time
where the time goes in v4:
time: 54.5 us; the launch traced here: 54.3 us
  Pallas kernels  51.1 us (94%)
  local copies, waits for them, and re-layouts  1.88 us (3%)
  between operations  1.31 us (2%)
    pallas_call x1, Pallas kernels, on_device(): pl.pallas_call(functools.partial(kernel, sizes), out_shape=jax.ShapeDtype...  51.1 us
    unnamed x1, local copies, waits for them, and re-layouts  1.88 us

profile of v4, /device:TPU:0, one launch (start us, length us, event | category | flops | bytes accessed | tf_op | source)
XLA Modules:
  0.0 54.3 jit_solution(16130829095947258651)
XLA Ops:
  1.3 51.1 %shard_map.118 = bf16[128,2048]{1,0:T(8,128)(2,1)} custom-call(s32[1,24]{1,0:T(1,128)} %holders_hbm.1, s32[1]{0:T(128)S(6)} %copy.14.prefix_ref, s32[1]{0:T(128)S(6)} %copy.15.count_ref, s32[1,24]{1,0:T(1,128)} %holders_hbm.1, s32[1,24]{1,0:T(1,128)} %blocks_hbm.1, bf16[6,128,512]{2,1,0:T(8,128)(2,1)} %pool_lat_hbm.1, bf16[6,64,128]{2,1,0:T(8,128)(2,1)} %pool_rope_hbm.1, ...), custom_call_target="tpu_custom_call" | custom-call | tf_op jit(solution)/shard_map/pallas_call | solution.py:598
  52.4 1.9 %copy.16 = bf16[128,2048]{1,0:T(8,128)(2,1)} copy(bf16[128,2048]{1,0:T(8,128)(2,1)} %shard_map.118) | data formatting | bytes 1048576
